TPU v7x, 32 devices: a whole 2x2x4 slice. The times are simulated.
32 devices in a mesh: groups: 2 (over y), rows: 4 (over z), cols: 4 (over x, core).
Axes of the slice: x: 2, y: 2, z: 4, core: 2. Of those that a mesh axis runs over, the one named last changes fastest.
Arguments:
- queries: bfloat16 [4096, 1024], P(('groups', 'rows', 'cols')), parts along dimension 0, may hold values from -4.25 to 4.25
- keys: bfloat16 [4096, 128], P(('groups', 'rows', 'cols')), parts along dimension 0, may hold values from -4.25 to 4.25
- values: bfloat16 [4096, 128], P(('groups', 'rows', 'cols')), parts along dimension 0, may hold values from -6 to 6
- positions: int32 [4096], P(('groups', 'rows', 'cols')), parts along dimension 0, may hold values from 0 to 2047, as said below
Outputs:
- attended: bfloat16 [4096, 1024], P(('groups', 'rows', 'cols')), parts along dimension 0
There are 2 independent parts, one for each index of `groups`. A program takes and returns all parts, laid end to end along the dimension named above; each array names one. Nothing has to cross between parts.
Inputs may be any that keep to these rules, and one draw needn't show every extreme that they name: `positions`: a permutation of 0 to 2047.
All inputs are finite; a program needn't handle non-finite values.
Results may differ from a plain program's by a relative error of at most 0.015.
Values may be sent and summed in bfloat16 or wider, within the bound.
A program may use at most 64 MiB of HBM per device.

v0:
```python
import math

import jax
import jax.numpy as jnp
from jax import lax
from jax.sharding import PartitionSpec as P

HEADS = 8
HEAD_DIM = 128


neg_fill = -1e30
tile_cap = 512


def make_absorb(query_heads, query_pos):
    scale = query_heads.shape[2] ** (-0.5)

    def absorb_tile(state, tile):
        key_tile, value_tile, pos_tile = tile
        run_max, run_sum, totals = state
        scores = (
            jnp.einsum("qhd,kd->qhk", query_heads, key_tile, preferred_element_type=jnp.float32)
            * scale
        )
        visible = pos_tile[None, None, :] <= query_pos[:, None, None]
        tile_max = jnp.max(jnp.where(visible, scores, neg_fill), axis=2)
        new_max = jnp.maximum(run_max, tile_max)
        weights = jnp.where(visible, jnp.exp(scores - new_max[:, :, None]), 0.0).astype(
            jnp.bfloat16
        )
        factor = jnp.exp(run_max - new_max)
        run_sum = run_sum * factor + jnp.sum(weights.astype(jnp.float32), axis=2)
        totals = totals * factor[:, :, None] + jnp.einsum(
            "qhk,kd->qhd", weights, value_tile, preferred_element_type=jnp.float32
        )
        return ((new_max, run_sum, totals), None)

    def absorb(carry, piece, start):
        key_part, value_part, key_pos = piece
        length = key_part.shape[0]
        tile_rows = math.gcd(length, tile_cap)
        tiles = length // tile_rows
        tiled = (
            key_part.reshape(tiles, tile_rows, key_part.shape[1]),
            value_part.reshape(tiles, tile_rows, value_part.shape[1]),
            key_pos.reshape(tiles, tile_rows),
        )
        carry, unused = lax.scan(absorb_tile, carry, tiled)
        return carry

    return absorb


def start_state(query_rows):
    return (
        jnp.full((query_rows, HEADS), neg_fill, jnp.float32),
        jnp.zeros((query_rows, HEADS), jnp.float32),
        jnp.zeros((query_rows, HEADS, HEAD_DIM), jnp.float32),
    )


def shards(queries, keys, values, positions):
    own_rows = queries.shape[0]
    query_heads = queries.reshape(own_rows, HEADS, HEAD_DIM)
    absorb = make_absorb(query_heads, positions)
    partial_value = absorb(
        start_state(own_rows),
        (
            lax.all_gather(keys, ("rows", "cols"), axis=0, tiled=True),
            lax.all_gather(values, ("rows", "cols"), axis=0, tiled=True),
            lax.all_gather(positions, ("rows", "cols"), axis=0, tiled=True),
        ),
        jnp.int32(0),
    )
    denominators = partial_value[1]
    numerators = partial_value[2]
    result = numerators / denominators[:, :, None]
    return result.astype(jnp.bfloat16).reshape(own_rows, HEADS * HEAD_DIM)


def solution(mesh):
    return jax.shard_map(
        shards,
        mesh=mesh,
        in_specs=(
            P(("groups", "rows", "cols"), None),
            P(("groups", "rows", "cols"), None),
            P(("groups", "rows", "cols"), None),
            P(("groups", "rows", "cols")),
        ),
        out_specs=P(("groups", "rows", "cols"), None),
        check_vma=False,
    )
```

profile of v0, /device:TPU:0, one launch (start us, length us, event | category | flops | bytes accessed | tf_op | source)
XLA Modules:
  0.0 78.9 jit_solution(12924049087476790847)
XLA Ops:
  0.0 0.0 copy-start
  0.0 24.9 %all_gather.10 = bf16[2048,128]{1,0:T(8,128)(2,1)S(1)} all-gather(bf16[128,128]{1,0:T(8,128)(2,1)} %param.7), channel_id=1, replica_groups=mesh['groups'=2,'rows'=4,'cols'=4] {'rows','cols'}, dimensions={0}, use_global_device_ids=true | all-gather | bytes 557056 | tf_op jit(solution)/shard_map/all_gather | solution.py:70
  24.9 20.5 %all_gather.11 = bf16[2048,128]{1,0:T(8,128)(2,1)} all-gather(bf16[128,128]{1,0:T(8,128)(2,1)} %param.8), channel_id=1, replica_groups=mesh['groups'=2,'rows'=4,'cols'=4] {'rows','cols'}, dimensions={0}, use_global_device_ids=true | all-gather | bytes 557056 | tf_op jit(solution)/shard_map/all_gather | solution.py:71
  45.4 1.1 %copy.12 = bf16[128,1024]{0,1:T(8,128)(2,1)S(1)} copy(bf16[128,1024]{1,0:T(8,128)(2,1)} %param.6) | data formatting | bytes 524288 | tf_op args[0]
  46.5 0.2 copy.13
  46.7 0.0 copy-done
  46.7 18.9 %all-gather = s32[16,1,128]{2,1,0:T(1,128)S(1)} all-gather(s32[1,1,128]{2,1,0:T(1,128)S(1)} %bitcast.53), channel_id=1, replica_groups=mesh['groups'=2,'rows'=4,'cols'=4] {'rows','cols'}, dimensions={0}, use_global_device_ids=true | all-gather | bytes 8704 | tf_op jit(solution)/shard_map/all_gather | solution.py:72
  65.6 0.5 broadcast.55
  66.1 0.7 reduce.3
  66.8 11.2 %while.15 = (s32[]{:T(128)}, f32[128,8]{0,1:T(8,128)S(1)}, f32[128,8]{0,1:T(8,128)S(1)}, f32[128,8,128]{2,0,1:T(8,128)S(1)}, s32[4,512]{1,0:T(4,128)S(1)}, /*ind...) while((s32[]{:T(128)}, f32[128,8]{0,1:T(8,128)S(1)}, ...), condition=%wide.region_3.4_spmd.clone, body=%wide.region_0.3_spmd.clone.sunk | while | flops 275715072 | bytes 8199297 | solution.py:49
  66.8 0.1 broadcast_compare_fusion.2
  67.0 0.5 fusion.24
  67.5 0.4 convert_reduce_fusion.2
  67.9 1.7 %convolution_add_fusion.2 = f32[128,8,128]{2,0,1:T(8,128)S(1)} fusion(f32[128,8,128]{2,0,1:T(8,128)S(1)} %get-tuple-element.202, f32[128,8]{0,1:T(8,128)S(1)} %get-tuple-element.187, pred[]{:T(512)S(6)} %compare.3, bf16[4,512,128]{2,1,0:T(8,128)(2,1)} %get-tuple-element.218, s32[]{:T(128)} %get-tuple-element.199, ...), kind=kOutput, calls=%fused_computation.7.clone.1 | convolution fusion | flops 136708096 | bytes 3351041 | tf_op jit(solution)/shard_map/while/body/eval_jaxpr/qhk,kd->qhd/dot_general | solution.py:34
  69.6 0.1 broadcast_compare_fusion.2
  69.8 0.5 fusion.24
  70.3 0.4 convert_reduce_fusion.2
  70.7 1.7 %convolution_add_fusion.2 = f32[128,8,128]{2,0,1:T(8,128)S(1)} fusion(f32[128,8,128]{2,0,1:T(8,128)S(1)} %get-tuple-element.202, f32[128,8]{0,1:T(8,128)S(1)} %get-tuple-element.187, pred[]{:T(512)S(6)} %compare.3, bf16[4,512,128]{2,1,0:T(8,128)(2,1)} %get-tuple-element.218, s32[]{:T(128)} %get-tuple-element.199, ...), kind=kOutput, calls=%fused_computation.7.clone.1 | convolution fusion | flops 136708096 | bytes 3351041 | tf_op jit(solution)/shard_map/while/body/eval_jaxpr/qhk,kd->qhd/dot_general | solution.py:34
  72.4 0.1 broadcast_compare_fusion.2
  72.6 0.5 fusion.24
  73.0 0.4 convert_reduce_fusion.2
  73.5 1.7 %convolution_add_fusion.2 = f32[128,8,128]{2,0,1:T(8,128)S(1)} fusion(f32[128,8,128]{2,0,1:T(8,128)S(1)} %get-tuple-element.202, f32[128,8]{0,1:T(8,128)S(1)} %get-tuple-element.187, pred[]{:T(512)S(6)} %compare.3, bf16[4,512,128]{2,1,0:T(8,128)(2,1)} %get-tuple-element.218, s32[]{:T(128)} %get-tuple-element.199, ...), kind=kOutput, calls=%fused_computation.7.clone.1 | convolution fusion | flops 136708096 | bytes 3351041 | tf_op jit(solution)/shard_map/while/body/eval_jaxpr/qhk,kd->qhd/dot_general | solution.py:34
  75.2 0.1 broadcast_compare_fusion.2
  75.4 0.5 fusion.24
  75.8 0.4 convert_reduce_fusion.2
  76.3 1.7 %convolution_add_fusion.2 = f32[128,8,128]{2,0,1:T(8,128)S(1)} fusion(f32[128,8,128]{2,0,1:T(8,128)S(1)} %get-tuple-element.202, f32[128,8]{0,1:T(8,128)S(1)} %get-tuple-element.187, pred[]{:T(512)S(6)} %compare.3, bf16[4,512,128]{2,1,0:T(8,128)(2,1)} %get-tuple-element.218, s32[]{:T(128)} %get-tuple-element.199, ...), kind=kOutput, calls=%fused_computation.7.clone.1 | convolution fusion | flops 136708096 | bytes 3351041 | tf_op jit(solution)/shard_map/while/body/eval_jaxpr/qhk,kd->qhd/dot_general | solution.py:34
  78.0 0.9 %copy_bitcast_fusion = bf16[128,1024]{1,0:T(8,128)(2,1)} fusion(f32[128,8,128]{2,0,1:T(8,128)S(1)} %get-tuple-element.53, f32[128,8]{0,1:T(8,128)S(1)} %get-tuple-element.54), kind=kLoop, calls=%fused_computation.23 | loop fusion | flops 262144 | bytes 790528 | tf_op jit(solution)/shard_map/reshape | solution.py:79
  (20 shorter events, 0.1 us)
Async XLA Ops:
  0.0 46.7 %copy-start = (s32[128]{0:T(128)S(1)}, s32[128]{0:T(128)}, u32[]{:S(2)}) copy-start(s32[128]{0:T(128)} %param.9) | copy-start | bytes 1540
where the time goes:
time: 79.2 us; the launch traced here: 78.9 us
  blocking collectives  64.3 us (81%)
  matrix products  8.48 us (11%)
  other arithmetic  3.95 us (5%)
  local copies, waits for them, and re-layouts  1.86 us (2%)
    all_gather x1, blocking collectives, shards(): lax.all_gather(keys, ('rows', 'cols'), axis=0, tiled=True)  24.9 us
    all_gather x1, blocking collectives, shards(): lax.all_gather(values, ('rows', 'cols'), axis=0, tiled=True)  20.5 us
    all_gather x1, blocking collectives, shards(): lax.all_gather(positions, ('rows', 'cols'), axis=0, tiled=True)  18.9 us
    dot_general x4, matrix products, absorb_tile(): jnp.einsum('qhk,kd->qhd', weights, value_tile, preferred_element_type=jnp...  6.65 us
    dot_general x4, matrix products, absorb_tile(): jnp.einsum('qhd,kd->qhk', query_heads, key_tile, preferred_element_type=j...  1.82 us
    reduce_sum x4, other arithmetic, absorb_tile(): run_sum = run_sum * factor + jnp.sum(weights.astype(jnp.float32), axis=2)  1.76 us

commit v1 on v0

v1 whole, which is shorter than its diff:
```python
import functools
import math

import jax
import jax.numpy as jnp
from jax import lax
from jax.experimental import pallas as pl
from jax.experimental.pallas import tpu as pltpu
from jax.sharding import PartitionSpec as P

HEADS = 8
HEAD_DIM = 128
NEG = -1e30
EXTRA = 16
HEAD_BLOCK = 2
MESH = pl.DeviceIdType.MESH


def kernel(rows, cols, q_ref, k_ref, v_ref, pos_ref, out_ref, buf, qs, qpos, run_max, acc, send_sem, recv_sem):
    length = k_ref.shape[0]
    pair = 2 if cols % 2 == 0 else 1
    wide = cols // pair
    count = rows * cols
    r, c = lax.axis_index("rows"), lax.axis_index("cols")
    x, core = c // pair, c % pair

    def slot(d, e, f):
        return (d * wide + e) * pair + f

    def row_at(d):
        return {"rows": lax.rem(r + d, rows), "cols": c}

    def wide_at(e):
        return {"rows": r, "cols": lax.rem(x + e, wide) * pair + core}

    def core_at():
        return {"rows": r, "cols": x * pair + (1 - core)}

    partners = [row_at(d) for d in range(1, rows)]
    partners += [wide_at(e) for e in range(1, wide)]
    partners += [core_at()] if pair == 2 else []
    barrier = pltpu.get_barrier_semaphore()
    for device in partners:
        pl.semaphore_signal(barrier, inc=1, device_id=device, device_id_type=MESH)

    position = pos_ref[...]
    buf[0, 0:length, :] = k_ref[...]
    buf[0, length : 2 * length, :] = v_ref[...]
    line = lax.broadcasted_iota(jnp.int32, (EXTRA, length), 0)
    digits = jnp.where(line == 0, position >> 7, jnp.where(line == 1, position & 127, 0))
    buf[0, 2 * length :, :] = digits.astype(jnp.float32).astype(jnp.bfloat16)

    pl.semaphore_wait(barrier, len(partners))

    copies = {}

    def send(source, target, device):
        copy = pltpu.make_async_remote_copy(
            src_ref=buf.at[source],
            dst_ref=buf.at[target],
            send_sem=send_sem.at[target],
            recv_sem=recv_sem.at[target],
            device_id=device,
            device_id_type=MESH,
        )
        copy.start()
        copies[target] = copy

    def to_core(d, e):
        if pair == 2:
            send(slot(d, e, 0), slot(d, e, 1), core_at())

    def spread(d):
        for e in range(1, wide):
            send(slot(d, 0, 0), slot(d, e, 0), wide_at(e))
        to_core(d, 0)

    def take_row(d):
        copies[slot(d, 0, 0)].wait_recv()
        spread(d)

    def take_wide(d):
        for e in range(1, wide):
            copies[slot(d, e, 0)].wait_recv()
            to_core(d, e)

    def take_core(d):
        if pair == 2:
            for e in range(wide):
                copies[slot(d, e, 1)].wait_recv()

    for d in range(1, rows):
        send(0, slot(d, 0, 0), row_at(d))
    spread(0)

    factor = math.log2(math.e) / math.sqrt(HEAD_DIM)
    for h in range(HEADS):
        scaled = q_ref[:, h * HEAD_DIM : (h + 1) * HEAD_DIM].astype(jnp.float32) * factor
        high = scaled.astype(jnp.bfloat16)
        low = (scaled - high.astype(jnp.float32)).astype(jnp.bfloat16)
        qs[h, :, 0:HEAD_DIM] = high
        qs[h, :, HEAD_DIM:] = low
    qpos[...] = jnp.transpose(jnp.broadcast_to(position.astype(jnp.float32), (length, length)))

    def absorb(first, number, fresh):
        block = buf[pl.ds(first, number)]
        key = block[:, 0:length].reshape(number * length, HEAD_DIM)
        value = block[:, length : 2 * length].reshape(number * length, HEAD_DIM)
        digit = block[:, 2 * length :].astype(jnp.float32)
        mine = qpos[...]
        bias = jnp.concatenate(
            [
                jnp.where(digit[i, 0:1] * 128.0 + digit[i, 1:2] <= mine, 0.0, NEG)
                for i in range(number)
            ],
            axis=1,
        )
        key = jnp.concatenate([key, key], axis=1)
        value = jnp.concatenate([value, jnp.ones_like(value)], axis=1)
        size = HEAD_BLOCK * length
        for h in range(0, HEADS, HEAD_BLOCK):
            query = qs[h : h + HEAD_BLOCK].reshape(size, 2 * HEAD_DIM)
            scores = lax.dot_general(
                query, key, (((1,), (1,)), ((), ())), preferred_element_type=jnp.float32
            )
            scores = (scores.reshape(HEAD_BLOCK, length, -1) + bias[None]).reshape(size, -1)
            top = jnp.max(scores, axis=1, keepdims=True)
            span = pl.ds(h * length, size)
            if not fresh:
                before = run_max[span, 0:1]
                top = jnp.maximum(before, top)
            weights = jnp.exp2(scores - top).astype(jnp.bfloat16)
            part = jnp.dot(weights, value, preferred_element_type=jnp.float32)
            if not fresh:
                part = acc[span, :] * jnp.exp2(before - top) + part
            acc[span, :] = part
            run_max[span, :] = jnp.broadcast_to(top, (size, 128))

    group = wide * pair
    if rows <= 4 and group <= 4:
        take_wide(0)
        for d in range(1, rows):
            take_row(d)
            take_wide(d - 1) if d > 1 else None
            if d > 1:
                take_core(d - 2)
                absorb((d - 2) * group, group, d == 2)
        if rows > 1:
            take_wide(rows - 1)
        for d in range(max(rows - 2, 0), rows):
            take_core(d)
            absorb(d * group, group, d == 0)
    else:
        take_wide(0)
        for d in range(1, rows):
            take_row(d)
        for d in range(1, rows):
            take_wide(d)
        for d in range(rows):
            take_core(d)
        number = math.gcd(count, 4)
        absorb(0, number, True)

        @pl.loop(1, count // number)
        def _(step):
            absorb(step * number, number, False)

    for h in range(HEADS):
        span = pl.ds(h * length, length)
        out_ref[:, h * HEAD_DIM : (h + 1) * HEAD_DIM] = (
            acc[span, 0:HEAD_DIM] / acc[span, HEAD_DIM:]
        ).astype(out_ref.dtype)
    for copy in copies.values():
        copy.wait_send()


def shards(rows, cols, queries, keys, values, positions):
    length = keys.shape[0]
    count = rows * cols
    return pl.pallas_call(
        functools.partial(kernel, rows, cols),
        out_shape=jax.ShapeDtypeStruct(queries.shape, jnp.bfloat16),
        in_specs=[pl.BlockSpec(memory_space=pltpu.VMEM)] * 4,
        out_specs=pl.BlockSpec(memory_space=pltpu.VMEM),
        scratch_shapes=[
            pltpu.VMEM((count, 2 * length + EXTRA, HEAD_DIM), jnp.bfloat16),
            pltpu.VMEM((HEADS, length, 2 * HEAD_DIM), jnp.bfloat16),
            pltpu.VMEM((length, length), jnp.float32),
            pltpu.VMEM((HEADS * length, 128), jnp.float32),
            pltpu.VMEM((HEADS * length, 2 * HEAD_DIM), jnp.float32),
            pltpu.SemaphoreType.DMA((count,)),
            pltpu.SemaphoreType.DMA((count,)),
        ],
        compiler_params=pltpu.CompilerParams(
            collective_id=0, has_side_effects=True, vmem_limit_bytes=40 * 1024 * 1024
        ),
    )(queries, keys, values, positions.reshape(1, length))


def solution(mesh):
    rows, cols = mesh.shape["rows"], mesh.shape["cols"]
    whole = P(("groups", "rows", "cols"), None)
    return jax.shard_map(
        functools.partial(shards, rows, cols),
        mesh=mesh,
        in_specs=(whole, whole, whole, P(("groups", "rows", "cols"))),
        out_specs=whole,
        check_vma=False,
    )
```

time: 79.2 us -> 24.4 us (0.31)
  blocking collectives: 64.3 us -> 0 us
  Pallas kernels: 0 us -> 20.2 us
  matrix products: 8.48 us -> 0 us
  other arithmetic: 3.95 us -> 0 us
  local copies, waits for them, and re-layouts: 1.86 us -> 3.82 us
    all_gather x3 -> x0, blocking collectives: 64.3 us -> none  [the longest x1 24.9 us: shards(): lax.all_gather(keys, ('rows', 'cols'), axis=0, tiled=True)]
    pallas_call x0 -> x1, Pallas kernels: none -> 20.2 us  [shards(): pl.pallas_call(functools.partial(kernel, rows, cols), out_shape=jax.Shape...]
    dot_general x8 -> x0, matrix products: 8.48 us -> none  [the longest x4 6.65 us: absorb_tile(): jnp.einsum('qhk,kd->qhd', weights, value_tile, preferred_element_type=jnp...]
    unnamed x4 -> x9, local copies, waits for them, and re-layouts: 1.3 us -> 3.82 us
    reduce_sum x4 -> x0, other arithmetic: 1.76 us -> none  [absorb_tile(): run_sum = run_sum * factor + jnp.sum(weights.astype(jnp.float32), axis=2)]
    reshape x1 -> x0, other arithmetic: 0.91 us -> none  [shards(): return result.astype(jnp.bfloat16).reshape(own_rows, HEADS * HEAD_DIM)]
where the time goes in v1:
time: 24.4 us; the launch traced here: 24.1 us
  Pallas kernels  20.2 us (83%)
  local copies, waits for them, and re-layouts  3.82 us (16%)
    pallas_call x1, Pallas kernels, shards(): pl.pallas_call(functools.partial(kernel, rows, cols), out_shape=jax.Shape...  20.2 us
    unnamed x9, local copies, waits for them, and re-layouts  3.82 us

profile of v1, /device:TPU:0, one launch (start us, length us, event | category | flops | bytes accessed | tf_op | source)
XLA Modules:
  0.0 24.1 jit_solution(6346730756045823658)
XLA Ops:
  0.0 0.0 copy-start.3
  0.0 0.7 %copy-done.3 = s32[128]{0:T(128)S(1)} copy-done((s32[128]{0:T(128)S(1)}, s32[128]{0:T(128)}, u32[]{:S(2)}) %copy-start.3) | copy-done | bytes 536
  0.7 0.0 copy-start
  0.7 0.9 %copy-done = bf16[128,1024]{1,0:T(8,128)(2,1)S(1)} copy-done((bf16[128,1024]{1,0:T(8,128)(2,1)S(1)}, bf16[128,1024]{1,0:T(8,128)(2,1)}, u32[]{:S(2)}) %copy-start) | copy-done | bytes 262168
  1.6 0.0 copy-start.1
  1.6 0.8 %copy-done.1 = bf16[128,128]{1,0:T(8,128)(2,1)S(1)} copy-done((bf16[128,128]{1,0:T(8,128)(2,1)S(1)}, bf16[128,128]{1,0:T(8,128)(2,1)}, u32[]{:S(2)}) %copy-start.1) | copy-done | bytes 32792
  2.4 0.0 copy-start.2
  2.4 0.8 %copy-done.2 = bf16[128,128]{1,0:T(8,128)(2,1)S(1)} copy-done((bf16[128,128]{1,0:T(8,128)(2,1)S(1)}, bf16[128,128]{1,0:T(8,128)(2,1)}, u32[]{:S(2)}) %copy-start.2) | copy-done | bytes 32792
  3.1 20.2 %shard_map.46 = bf16[128,1024]{1,0:T(8,128)(2,1)S(1)} custom-call(bf16[128,1024]{1,0:T(8,128)(2,1)S(1)} %copy-done, bf16[128,128]{1,0:T(8,128)(2,1)S(1)} %copy-done.1, bf16[128,128]{1,0:T(8,128)(2,1)S(1)} %copy-done.2, s32[1,128]{1,0:T(1,128)S(1)} %bitcast.1), custom_call_target="tpu_custom_call" | custom-call | tf_op jit(solution)/shard_map/pallas_call | solution.py:180
  23.4 0.7 %copy.6 = bf16[128,1024]{1,0:T(8,128)(2,1)} copy(bf16[128,1024]{1,0:T(8,128)(2,1)S(1)} %shard_map.46) | data formatting | bytes 524288
Async XLA Ops:
  0.0 0.7 %copy-start.3 = (s32[128]{0:T(128)S(1)}, s32[128]{0:T(128)}, u32[]{:S(2)}) copy-start(s32[128]{0:T(128)} %param.7) | copy-start | bytes 1540
  0.7 0.9 %copy-start = (bf16[128,1024]{1,0:T(8,128)(2,1)S(1)}, bf16[128,1024]{1,0:T(8,128)(2,1)}, u32[]{:S(2)}) copy-start(bf16[128,1024]{1,0:T(8,128)(2,1)} %q_ref.1) | copy-start | bytes 786436
  1.6 0.8 %copy-start.1 = (bf16[128,128]{1,0:T(8,128)(2,1)S(1)}, bf16[128,128]{1,0:T(8,128)(2,1)}, u32[]{:S(2)}) copy-start(bf16[128,128]{1,0:T(8,128)(2,1)} %k_ref.1) | copy-start | bytes 98308
  2.4 0.8 %copy-start.2 = (bf16[128,128]{1,0:T(8,128)(2,1)S(1)}, bf16[128,128]{1,0:T(8,128)(2,1)}, u32[]{:S(2)}) copy-start(bf16[128,128]{1,0:T(8,128)(2,1)} %v_ref.1) | copy-start | bytes 98308

commit v2 on v1

--- a/solution.py
+++ b/solution.py
@@ -16,16 +16,35 @@
 MESH = pl.DeviceIdType.MESH
 
 
-def kernel(rows, cols, q_ref, k_ref, v_ref, pos_ref, out_ref, buf, qs, qpos, run_max, acc, send_sem, recv_sem):
-    length = k_ref.shape[0]
+def kernel(rows, cols, q_hbm, k_hbm, v_hbm, pos_hbm, out_ref, q_ref, pos_ref, buf, qs, qpos, run_max, acc, load_sem, send_sem, recv_sem):
+    length = k_hbm.shape[0]
+    loads = [
+        pltpu.make_async_copy(source, target, load_sem.at[i])
+        for i, (source, target) in enumerate(
+            (
+                (pos_hbm, pos_ref),
+                (k_hbm, buf.at[0, pl.ds(0, length)]),
+                (v_hbm, buf.at[0, pl.ds(length, length)]),
+                (q_hbm, q_ref),
+            )
+        )
+    ]
+    for load in loads:
+        load.start()
     pair = 2 if cols % 2 == 0 else 1
     wide = cols // pair
     count = rows * cols
     r, c = lax.axis_index("rows"), lax.axis_index("cols")
     x, core = c // pair, c % pair
 
+    relay = rows == 4 and wide == 2 and pair == 2
+    if relay:
+        order = [(0, 0), (1, 0), (3, 0), (0, 1), (2, 0), (1, 1), (3, 1), (2, 1)]
+    else:
+        order = [(d, e) for d in range(rows) for e in range(wide)]
+
     def slot(d, e, f):
-        return (d * wide + e) * pair + f
+        return order.index((d, e)) * pair + f
 
     def row_at(d):
         return {"rows": lax.rem(r + d, rows), "cols": c}
@@ -33,23 +52,29 @@
     def wide_at(e):
         return {"rows": r, "cols": lax.rem(x + e, wide) * pair + core}
 
+    def across_at(d):
+        return {"rows": lax.rem(r + d, rows), "cols": lax.rem(x + 1, wide) * pair + core}
+
     def core_at():
         return {"rows": r, "cols": x * pair + (1 - core)}
 
-    partners = [row_at(d) for d in range(1, rows)]
+    near = (1, 3) if relay else range(1, rows)
+    partners = [row_at(d) for d in near]
+    partners += [across_at(d) for d in near] if relay else []
     partners += [wide_at(e) for e in range(1, wide)]
     partners += [core_at()] if pair == 2 else []
     barrier = pltpu.get_barrier_semaphore()
     for device in partners:
         pl.semaphore_signal(barrier, inc=1, device_id=device, device_id_type=MESH)
 
+    loads[0].wait()
     position = pos_ref[...]
-    buf[0, 0:length, :] = k_ref[...]
-    buf[0, length : 2 * length, :] = v_ref[...]
     line = lax.broadcasted_iota(jnp.int32, (EXTRA, length), 0)
     digits = jnp.where(line == 0, position >> 7, jnp.where(line == 1, position & 127, 0))
     buf[0, 2 * length :, :] = digits.astype(jnp.float32).astype(jnp.bfloat16)
 
+    loads[1].wait()
+    loads[2].wait()
     pl.semaphore_wait(barrier, len(partners))
 
     copies = {}
@@ -84,15 +109,15 @@
             copies[slot(d, e, 0)].wait_recv()
             to_core(d, e)
 
-    def take_core(d):
+    def take_core(d, e):
         if pair == 2:
-            for e in range(wide):
-                copies[slot(d, e, 1)].wait_recv()
-
-    for d in range(1, rows):
+            copies[slot(d, e, 1)].wait_recv()
+
+    for d in near:
         send(0, slot(d, 0, 0), row_at(d))
     spread(0)
 
+    loads[3].wait()
     factor = math.log2(math.e) / math.sqrt(HEAD_DIM)
     for h in range(HEADS):
         scaled = q_ref[:, h * HEAD_DIM : (h + 1) * HEAD_DIM].astype(jnp.float32) * factor
@@ -136,20 +161,32 @@
             acc[span, :] = part
             run_max[span, :] = jnp.broadcast_to(top, (size, 128))
 
-    group = wide * pair
-    if rows <= 4 and group <= 4:
+    if relay:
+        take_core(0, 0)
+        absorb(0, 2, True)
+        copies[slot(1, 0, 0)].wait_recv()
+        send(slot(1, 0, 0), slot(2, 1, 0), across_at(1))
+        send(slot(1, 0, 0), slot(2, 0, 0), row_at(1))
+        spread(1)
+        take_row(3)
         take_wide(0)
-        for d in range(1, rows):
-            take_row(d)
-            take_wide(d - 1) if d > 1 else None
-            if d > 1:
-                take_core(d - 2)
-                absorb((d - 2) * group, group, d == 2)
-        if rows > 1:
-            take_wide(rows - 1)
-        for d in range(max(rows - 2, 0), rows):
-            take_core(d)
-            absorb(d * group, group, d == 0)
+        take_core(1, 0)
+        take_core(3, 0)
+        absorb(2, 4, False)
+        take_core(0, 1)
+        absorb(6, 2, False)
+        copies[slot(2, 0, 0)].wait_recv()
+        to_core(2, 0)
+        take_wide(1)
+        take_wide(3)
+        take_core(2, 0)
+        absorb(8, 2, False)
+        take_wide(2)
+        take_core(1, 1)
+        take_core(3, 1)
+        absorb(10, 4, False)
+        take_core(2, 1)
+        absorb(14, 2, False)
     else:
         take_wide(0)
         for d in range(1, rows):
@@ -157,7 +194,8 @@
         for d in range(1, rows):
             take_wide(d)
         for d in range(rows):
-            take_core(d)
+            for e in range(wide):
+                take_core(d, e)
         number = math.gcd(count, 4)
         absorb(0, number, True)
 
@@ -180,19 +218,22 @@
     return pl.pallas_call(
         functools.partial(kernel, rows, cols),
         out_shape=jax.ShapeDtypeStruct(queries.shape, jnp.bfloat16),
-        in_specs=[pl.BlockSpec(memory_space=pltpu.VMEM)] * 4,
+        in_specs=[pl.BlockSpec(memory_space=pltpu.HBM)] * 4,
         out_specs=pl.BlockSpec(memory_space=pltpu.VMEM),
         scratch_shapes=[
+            pltpu.VMEM(queries.shape, jnp.bfloat16),
+            pltpu.VMEM((1, length), jnp.int32),
             pltpu.VMEM((count, 2 * length + EXTRA, HEAD_DIM), jnp.bfloat16),
             pltpu.VMEM((HEADS, length, 2 * HEAD_DIM), jnp.bfloat16),
             pltpu.VMEM((length, length), jnp.float32),
             pltpu.VMEM((HEADS * length, 128), jnp.float32),
             pltpu.VMEM((HEADS * length, 2 * HEAD_DIM), jnp.float32),
+            pltpu.SemaphoreType.DMA((4,)),
             pltpu.SemaphoreType.DMA((count,)),
             pltpu.SemaphoreType.DMA((count,)),
         ],
         compiler_params=pltpu.CompilerParams(
-            collective_id=0, has_side_effects=True, vmem_limit_bytes=40 * 1024 * 1024
+            collective_id=0, has_side_effects=True, vmem_limit_bytes=56 * 1024 * 1024
         ),
     )(queries, keys, values, positions.reshape(1, length))
 

time: 24.4 us -> 21.5 us (0.88)
  local copies, waits for them, and re-layouts: 3.82 us -> 1.67 us
  Pallas kernels: 20.2 us -> 19.7 us
    unnamed x9 -> x1, local copies, waits for them, and re-layouts: 3.82 us -> 1.67 us
    pallas_call x1, Pallas kernels: 20.2 us -> 19.7 us  [shards(): pl.pallas_call(functools.partial(kernel, rows, cols), out_shape=jax.Shape...]
where the time goes in v2:
time: 21.5 us; the launch traced here: 21.4 us
  Pallas kernels  19.7 us (92%)
  local copies, waits for them, and re-layouts  1.67 us (8%)
    pallas_call x1, Pallas kernels, shards(): pl.pallas_call(functools.partial(kernel, rows, cols), out_shape=jax.Shape...  19.7 us
    unnamed x1, local copies, waits for them, and re-layouts  1.67 us

profile of v2, /device:TPU:0, one launch (start us, length us, event | category | flops | bytes accessed | tf_op | source)
XLA Modules:
  0.0 21.4 jit_solution(11537630805082409305)
XLA Ops:
  0.0 19.7 %shard_map.46 = bf16[128,1024]{1,0:T(8,128)(2,1)} custom-call(bf16[128,1024]{1,0:T(8,128)(2,1)} %q_hbm.1, bf16[128,128]{1,0:T(8,128)(2,1)} %k_hbm.1, bf16[128,128]{1,0:T(8,128)(2,1)} %v_hbm.1, s32[1,128]{1,0:T(1,128)} %bitcast.1), custom_call_target="tpu_custom_call" | custom-call | tf_op jit(solution)/shard_map/pallas_call | solution.py:218
  19.7 1.7 %copy.6 = bf16[128,1024]{1,0:T(8,128)(2,1)} copy(bf16[128,1024]{1,0:T(8,128)(2,1)} %shard_map.46) | data formatting | bytes 524288

commit v3 on v2

--- a/solution.py
+++ b/solution.py
@@ -162,8 +162,6 @@
             run_max[span, :] = jnp.broadcast_to(top, (size, 128))
 
     if relay:
-        take_core(0, 0)
-        absorb(0, 2, True)
         copies[slot(1, 0, 0)].wait_recv()
         send(slot(1, 0, 0), slot(2, 1, 0), across_at(1))
         send(slot(1, 0, 0), slot(2, 0, 0), row_at(1))
@@ -172,21 +170,19 @@
         take_wide(0)
         take_core(1, 0)
         take_core(3, 0)
-        absorb(2, 4, False)
+        take_core(0, 0)
         take_core(0, 1)
-        absorb(6, 2, False)
+        absorb(0, 8, True)
         copies[slot(2, 0, 0)].wait_recv()
         to_core(2, 0)
         take_wide(1)
         take_wide(3)
         take_core(2, 0)
-        absorb(8, 2, False)
         take_wide(2)
         take_core(1, 1)
         take_core(3, 1)
-        absorb(10, 4, False)
         take_core(2, 1)
-        absorb(14, 2, False)
+        absorb(8, 8, False)
     else:
         take_wide(0)
         for d in range(1, rows):

time: 21.5 us -> 20.2 us (0.940)
  Pallas kernels: 19.7 us -> 18.4 us
    pallas_call x1, Pallas kernels: 19.7 us -> 18.4 us  [shards(): pl.pallas_call(functools.partial(kernel, rows, cols), out_shape=jax.Shape...]
where the time goes in v3:
time: 20.2 us; the launch traced here: 20.1 us
  Pallas kernels  18.4 us (91%)
  local copies, waits for them, and re-layouts  1.67 us (8%)
    pallas_call x1, Pallas kernels, shards(): pl.pallas_call(functools.partial(kernel, rows, cols), out_shape=jax.Shape...  18.4 us
    unnamed x1, local copies, waits for them, and re-layouts  1.67 us

profile of v3, /device:TPU:0, one launch (start us, length us, event | category | flops | bytes accessed | tf_op | source)
XLA Modules:
  0.0 20.1 jit_solution(5272776018228230535)
XLA Ops:
  0.0 18.4 %shard_map.46 = bf16[128,1024]{1,0:T(8,128)(2,1)} custom-call(bf16[128,1024]{1,0:T(8,128)(2,1)} %q_hbm.1, bf16[128,128]{1,0:T(8,128)(2,1)} %k_hbm.1, bf16[128,128]{1,0:T(8,128)(2,1)} %v_hbm.1, s32[1,128]{1,0:T(1,128)} %bitcast.1), custom_call_target="tpu_custom_call" | custom-call | tf_op jit(solution)/shard_map/pallas_call | solution.py:214
  18.4 1.7 %copy.6 = bf16[128,1024]{1,0:T(8,128)(2,1)} copy(bf16[128,1024]{1,0:T(8,128)(2,1)} %shard_map.46) | data formatting | bytes 524288
